TPU v7x, 512 devices: a whole 4x8x8 slice. The times are simulated.
512 devices in a mesh: rows: 16 (over z, core), cols: 32 (over x, y).
Axes of the slice: x: 4, y: 8, z: 8, core: 2. Of those that a mesh axis runs over, the one named last changes fastest.
Arguments:
- left_query: bfloat16 [32, 4096, 256], P('rows', 'cols'), parts along dimension 0, may hold values from -16 to 16
- left_value: bfloat16 [32, 4096, 256], P('rows', 'cols'), parts along dimension 0, may hold values from -6 to 6
- right_key: bfloat16 [32, 4096, 256], P('rows', 'cols'), parts along dimension 0, may hold values from -16 to 16
- right_value: bfloat16 [32, 4096, 256], P('rows', 'cols'), parts along dimension 0, may hold values from -6 to 6
- bound: int32 [32], P('rows'), parts along dimension 0, may hold values from 0 to 31
Outputs:
- left_out: bfloat16 [32, 4096, 256], P('rows', 'cols'), parts along dimension 0
- right_out: bfloat16 [32, 4096, 256], P('rows', 'cols'), parts along dimension 0
There are 16 independent parts, one for each index of `rows`. A program takes and returns all parts, laid end to end along the dimension named above; each array names one. Nothing has to cross between parts.
All inputs are finite; a program needn't handle non-finite values.
Results may differ from a plain program's by a relative error of at most 0.0045.
Values may be sent and summed in bfloat16 or wider, within the bound.
A program may use at most 64 MiB of HBM per device.

v0:
```python
import math

import jax
import jax.numpy as jnp
from jax import lax
from jax.sharding import PartitionSpec as P


def in_one_piece(arrays, axis, dim, along):
    both = jnp.concatenate(arrays, axis=along)
    filled, at, done = (lax.all_gather(both, axis, axis=dim, tiled=True), 0, [])
    for a in arrays:
        done.append(lax.slice_in_dim(filled, at, at + a.shape[along], axis=along))
        at += a.shape[along]
    return tuple(done)


def online_update(carry, scores, valid, values):
    run_max, run_total, run_sum = carry
    masked = jnp.where(valid, scores, -1e30)
    new_max = jnp.maximum(run_max, jnp.max(masked, axis=-1))
    weights = jnp.where(valid, jnp.exp(scores - new_max[:, :, None]), 0.0)
    new_total = jnp.sum(weights, axis=-1)
    product = jnp.einsum(
        "rij,rjd->rid", weights.astype(jnp.bfloat16), values, preferred_element_type=jnp.float32
    )
    return (new_max, new_total, product)


def body(left_query, left_value, right_key, right_value, bound):
    rows_n, width, depth = left_query.shape
    ncols = lax.axis_size("cols")
    here = lax.axis_index("cols")
    total_len = width * ncols
    scale = 1.0 / math.sqrt(depth)
    own_pos = here * width + jnp.arange(width, dtype=jnp.int32)
    own_block = own_pos // width
    reach = bound[:, None, None]
    widest = jnp.max(bound)
    initial = (
        jnp.full((rows_n, width), -1e30, jnp.float32),
        jnp.zeros((rows_n, width), jnp.float32),
        jnp.zeros((rows_n, width, depth), jnp.float32),
    )

    def make_step(mine, lower_side):

        def compute(carry, piece):
            other_rows, other_values = piece
            count = other_rows.shape[1]
            other_pos = jnp.arange(count, dtype=jnp.int32)
            other_block = other_pos // width
            scores = (
                jnp.einsum("rid,rjd->rij", mine, other_rows, preferred_element_type=jnp.float32)
                * scale
            )
            if lower_side:
                valid = (
                    (other_pos[None, None, :] <= own_pos[None, :, None])
                    & (other_pos >= 0)[None, None, :]
                    & (own_block[None, :, None] - other_block[None, None, :] <= reach)
                )
            else:
                valid = (
                    (other_pos[None, None, :] >= own_pos[None, :, None])
                    & (other_pos < total_len)[None, None, :]
                    & (other_block[None, None, :] - own_block[None, :, None] <= reach)
                )
            return online_update(carry, scores, valid, other_values)

        def step(carry, piece, start):
            count = piece[0].shape[1]
            lowest = start // width
            highest = (start + count - 1) // width
            if lower_side:
                needed = (jnp.maximum(lowest, 0) <= here) & (
                    here - jnp.minimum(highest, here) <= widest
                )
            else:
                needed = (jnp.minimum(highest, ncols - 1) >= here) & (
                    jnp.maximum(lowest, here) - here <= widest
                )
            return lax.cond(needed, lambda c: compute(c, piece), lambda c: c, carry)

        return step

    left_step = make_step(left_query, True)
    right_step = make_step(right_key, False)
    left_carry = left_step(
        initial, in_one_piece((right_key, right_value), "cols", 1, 0), jnp.int32(0)
    )
    right_carry = right_step(
        initial, in_one_piece((left_query, left_value), "cols", 1, 0), jnp.int32(0)
    )
    left_out = (left_carry[2] / left_carry[1][:, :, None]).astype(jnp.bfloat16)
    right_out = (right_carry[2] / right_carry[1][:, :, None]).astype(jnp.bfloat16)
    return (left_out, right_out)


def solution(mesh):
    placed = (
        P("rows", "cols", None),
        P("rows", "cols", None),
        P("rows", "cols", None),
        P("rows", "cols", None),
        P("rows"),
    )
    return jax.shard_map(
        body,
        mesh=mesh,
        in_specs=placed,
        out_specs=(P("rows", "cols", None), P("rows", "cols", None)),
        check_vma=False,
    )
```

profile of v0, /device:TPU:1, one launch (start us, length us, event | category | flops | bytes accessed | tf_op | source)
XLA Modules:
  0.0 239.4 jit_solution(17517483206455877653)
XLA Ops:
  7.2 0.0 all-gather.5.cloned.1.call-start
  7.2 1.7 pad_maximum_fusion.1
  8.9 0.0 all-gather.5.cloned.1.call-update
  8.9 0.0 all-gather.3.cloned.1.call-start
  9.0 1.7 pad_maximum_fusion
  10.7 0.0 all-gather.3.cloned.1.call-update
  10.7 1.3 reduce_max.27
  13.3 106.4 %all-gather.5.cloned.1.call-done = bf16[4,4096,256]{2,1,0:T(8,128)(2,1)} async-done(((bf16[4,128,256]{2,1,0:T(8,128)(2,1)}), bf16[4,4096,256]{2,1,0:T(8,128)(2,1)}) %all-gather.5.cloned.1.call-update) | async-done | bytes 8388624 | tf_op jit(solution)/shard_map/all_gather | solution.py:11
  119.7 0.0 copy-start
  119.7 8.1 %conditional.3 = (f32[2,128]{1,0:T(2,128)S(1)}, f32[2,128,256]{2,1,0:T(8,128)S(1)}) conditional(s32[]{:T(128)} %convert_element_type.20, () %tuple.26, (s32[128]{0:T(128)S(1)}, s32[128]{0:T(128)S(1)}, s32[2,1,1]{0,2,1:T(1,128)}, bf16[2,128,256]{2,1,0:T(8,128)(2,1)}, bf16[4,4096,256]{2,1,0:T(8,128)(2,1)}, ...), branch_computations={%region_5.6_spmd, %region_6.9_spmd} | conditional | flops 1091079936 | bytes 57065604 | solution.py:83
  119.7 0.4 fusion.25
  120.1 0.0 slice-start.2
  120.2 0.2 broadcast_subtract_fusion.1
  120.4 0.0 slice-start.3
  120.4 0.0 copy-start.1
  120.4 4.1 %select_reduce_fusion.1 = (f32[2,128]{1,0:T(2,128)S(1)}, f32[2,128,4096]{2,1,0:T(8,128)S(1)}) fusion(s32[128,4096]{1,0:T(8,128)S(1)} %broadcast_subtract_fusion.1, s32[2]{0:T(128)} %bitcast.11, pred[128,4096]{1,0:T(8,128)(4,1)S(1)} %fusion.25, bf16[2,128,256]{2,1,0:T(8,128)(2,1)} %get-tuple-element.33, bf16[4,4096,256]{2,1,0:T(8,128)(2,1)} %get-tuple-element.49), kind=kOutput, calls=%fused_computation.30 | convolution fusion | flops 542113536 | bytes 11142656 | tf_op jit(solution)/shard_map/cond/branch_1_fun/rid,rjd->rij/dot_general | solution.py:54
  124.5 0.0 slice-done.2
  124.6 0.5 slice-done.3
  125.0 0.0 copy-done.1
  125.0 1.3 fusion.15
  126.3 1.5 fusion.19
  127.8 0.8 divide_convert_fusion
  128.6 95.3 %all-gather.3.cloned.1.call-done = bf16[4,4096,256]{2,1,0:T(8,128)(2,1)} async-done(((bf16[4,128,256]{2,1,0:T(8,128)(2,1)}), bf16[4,4096,256]{2,1,0:T(8,128)(2,1)}) %all-gather.3.cloned.1.call-update) | async-done | bytes 8388624 | tf_op jit(solution)/shard_map/all_gather | solution.py:11
  223.9 0.0 copy-done
  223.9 8.0 %conditional.2 = (f32[2,128]{1,0:T(2,128)S(1)}, f32[2,128,256]{2,1,0:T(8,128)S(1)}) conditional(s32[]{:T(128)} %convert_element_type.18, () %tuple.24, (s32[128]{0:T(128)S(1)}, s32[128]{0:T(128)S(1)}, s32[2,1,1]{0,2,1:T(1,128)}, bf16[2,128,256]{2,1,0:T(8,128)(2,1)S(1)}, bf16[4,4096,256]{2,1,0:T(8,128)(2,1)}, ...), branch_computations={%region_1.2_spmd, %region_2.5_spmd} | conditional | flops 1090551552 | bytes 57057412 | solution.py:83
  223.9 0.4 iota_compare_fusion
  224.2 0.0 slice-start
  224.3 0.2 broadcast_subtract_fusion
  224.5 0.0 slice-start.1
  224.5 0.0 copy-start.2
  224.5 4.1 %select_reduce_fusion = (f32[2,128]{1,0:T(2,128)S(1)}, f32[2,128,4096]{2,1,0:T(8,128)S(1)}) fusion(s32[128,4096]{1,0:T(8,128)S(1)} %broadcast_subtract_fusion, s32[2]{0:T(128)} %bitcast.14, pred[128,4096]{1,0:T(8,128)(4,1)S(1)} %iota_compare_fusion, bf16[2,128,256]{2,1,0:T(8,128)(2,1)S(1)} %get-tuple-element.27, bf16[4,4096,256]{2,1,0:T(8,128)(2,1)} %get-tuple-element.47), kind=kOutput, calls=%fused_computation.5 | convolution fusion | flops 542113536 | bytes 11142656 | tf_op jit(solution)/shard_map/cond/branch_1_fun/rid,rjd->rij/dot_general | solution.py:54
  228.7 0.0 slice-done
  228.7 0.4 slice-done.1
  229.1 0.0 copy-done.2
  229.1 1.3 fusion
  230.4 1.5 fusion.4
  231.8 0.8 divide_convert_fusion.1
  (8 shorter events, 0.0 us)
Async XLA Ops:
  7.2 112.5 %all-gather.5.cloned.1.call-start = ((), (), s32[]{:S(2)}) async-start(), calls=%async_computation.1 | async-start | bytes 8650752 | tf_op jit(solution)/shard_map/all_gather | solution.py:11
  8.9 214.9 %all-gather.3.cloned.1.call-start = ((), (), s32[]{:S(2)}) async-start(), calls=%async_computation | async-start | bytes 8650752 | tf_op jit(solution)/shard_map/all_gather | solution.py:11
  119.7 104.2 %copy-start = (bf16[2,128,256]{2,1,0:T(8,128)(2,1)S(1)}, bf16[2,128,256]{2,1,0:T(8,128)(2,1)}, u32[]{:S(2)}) copy-start(bf16[2,128,256]{2,1,0:T(8,128)(2,1)} %param.9) | copy-start | bytes 393220
  120.1 4.4 %slice-start.2 = ((s8[8388608]{0:T(1024)(128)(4,1)}), s8[4194304]{0:T(1024)(128)(4,1)S(1)}, s32[]{:S(2)}) async-start(s8[8388608]{0:T(1024)(128)(4,1)} %bitcast.7), calls=%async_computation.4 | async-start | bytes 8388608 | tf_op jit(solution)/shard_map/cond
  120.4 4.6 %slice-start.3 = ((s8[8388608]{0:T(1024)(128)(4,1)}), s8[4194304]{0:T(1024)(128)(4,1)S(1)}, s32[]{:S(2)}) async-start(s8[8388608]{0:T(1024)(128)(4,1)} %bitcast.7), calls=%async_computation.5 | async-start | bytes 8388608 | tf_op jit(solution)/shard_map/cond
  120.4 4.6 %copy-start.1 = (s32[2,1,1]{0,2,1:T(1,128)S(1)}, s32[2,1,1]{0,2,1:T(1,128)}, u32[]{:S(2)}) copy-start(s32[2,1,1]{0,2,1:T(1,128)} %get-tuple-element.32) | copy-start | bytes 28 | tf_op jit(solution)/shard_map/cond
  224.2 4.4 %slice-start = ((s8[8388608]{0:T(1024)(128)(4,1)}), s8[4194304]{0:T(1024)(128)(4,1)S(1)}, s32[]{:S(2)}) async-start(s8[8388608]{0:T(1024)(128)(4,1)} %bitcast.5), calls=%async_computation.2 | async-start | bytes 8388608 | tf_op jit(solution)/shard_map/cond
  224.5 4.5 %slice-start.1 = ((s8[8388608]{0:T(1024)(128)(4,1)}), s8[4194304]{0:T(1024)(128)(4,1)S(1)}, s32[]{:S(2)}) async-start(s8[8388608]{0:T(1024)(128)(4,1)} %bitcast.5), calls=%async_computation.3 | async-start | bytes 8388608 | tf_op jit(solution)/shard_map/cond
  224.5 4.5 %copy-start.2 = (s32[2,1,1]{0,2,1:T(1,128)S(1)}, s32[2,1,1]{0,2,1:T(1,128)}, u32[]{:S(2)}) copy-start(s32[2,1,1]{0,2,1:T(1,128)} %get-tuple-element.26) | copy-start | bytes 28 | tf_op jit(solution)/shard_map/cond
Sparse Core Ops, SparseCore 0:
  11.2 108.4 all-gather.4
  122.9 100.9 all-gather.2
where the time goes:
time: 240 us; the launch traced here: 239 us
  waiting for transfers between devices  202 us (84%)
  between operations  15.4 us (6%)
  matrix products  10.8 us (4%)
  other arithmetic  10.5 us (4%)
    all_gather x2, waiting for transfers between devices, in_one_piece(): filled, at, done = (lax.all_gather(both, axis, axis=dim, tiled=True), 0, [])  202 us
    dot_general x2, matrix products, compute(): jnp.einsum('rid,rjd->rij', mine, other_rows, preferred_element_type=jnp.f...  8.21 us
  transfers between devices with their start and end apart: 2, of which 2 were waited for; matrix products, arithmetic and copies ran while one was open for 5% of the time, Pallas kernels for 0%

commit v1 on v0

v1 whole, which is shorter than its diff:
```python
import jax
import jax.numpy as jnp
from jax import lax
from jax.experimental import pallas as pl
from jax.experimental.pallas import tpu as pltpu
from jax.sharding import PartitionSpec as P

MESH = pl.DeviceIdType.MESH
F32 = jnp.float32
BF16 = jnp.bfloat16

NX, NY = 4, 8
T, D = 128, 256
STAT = 16
MSG = D + STAT
NEVER = -(2.0**100)
FAR = 1 << 28
SCALE = 1.4426950408889634 / 16.0

AP, B1P, B1M, B2, AX = 0, 1, 2, 3, 4
PAX, PAP, PBF, PBP, PBM = 14, 17, 18, 19, 20
KINDS = 21


def kernel(
    bound_ref, lq, lv, rk, rv, lo, ro,
    ak, av, bk, bv, raw, pa_w, pb_w, sa, sb, oa, ob, stat_a, stat_b,
    pa, ra, passed, rap, pb, rb, send, recv, local,
):
    row = lax.axis_index("rows")
    col = lax.axis_index("cols")
    x, y = col // NY, col % NY

    def at(nx, ny):
        return (row, nx * NY + ny)

    def step_y(d):
        return lax.rem(y + d + NY, NY)

    odd = lax.rem(y, 2)
    partner = [step_y(1 - 2 * odd), step_y(2 * odd - 1)]
    up, down = at(x, step_y(2)), at(x, step_y(-2))
    mate = [at(x, partner[0]), at(x, partner[1])]
    across = [at(lax.rem(x + d, NX), y) for d in (1, 2, 3)]

    keys_a, keys_b = (lq.at[0], rk.at[1]), (rk.at[0], lq.at[1])
    vals_a, vals_b = (lv.at[0], rv.at[1]), (rv.at[0], lv.at[1])
    out_a, out_b = (lo.at[0], ro.at[1]), (ro.at[0], lo.at[1])
    lines = [NX - x, x + 1]

    barrier = pltpu.get_barrier_semaphore()
    for device in [up, down] + mate + across:
        pl.semaphore_signal(barrier, inc=1, device_id=device, device_id_type=MESH)

    copies = []
    for t in range(2):
        for src, dst in (
            (keys_a[t], ak.at[t, 0, pl.ds(0, T)]),
            (keys_b[t], bk.at[t, pl.ds(0, T)]),
            (vals_a[t], raw.at[t, 0]),
            (vals_b[t], raw.at[t, 1]),
        ):
            copies.append(pltpu.make_async_copy(src, dst, local.at[len(copies)]))
            copies[-1].start()
    for copy in copies:
        copy.wait()
    for t in range(2):
        av[t, 0, 0] = raw[t, 0].astype(F32).T.astype(BF16)
        bv[t, 0] = raw[t, 1].astype(F32).T.astype(BF16)

    pl.semaphore_wait(barrier, 7)

    def message(t, number, src, dst, device):
        n = t * KINDS + number
        return pltpu.make_async_remote_copy(
            src_ref=src, dst_ref=dst, send_sem=send.at[n], recv_sem=recv.at[n],
            device_id=device, device_id_type=MESH,
        )

    def line(t, d):
        return at(x - d, y) if t == 0 else at(x + d, y)

    def line_in(t, d):
        return x - d >= 0 if t == 0 else x + d < NX

    def ap(t, kv):
        if kv == 0:
            return message(t, AP, ak.at[t, 0, pl.ds(0, T)], ak.at[t, 0, pl.ds(T, T)], mate[t])
        return message(t, 7 + AP, av.at[t, 0, 0], av.at[t, 0, 1], mate[t])

    def b_slot(t, kv, s):
        return bk.at[t, pl.ds(s * T, T)] if kv == 0 else bv.at[t, s]

    def b1p(t, kv):
        return message(t, 7 * kv + B1P, b_slot(t, kv, 0), b_slot(t, kv, 1), up)

    def b1m(t, kv):
        return message(t, 7 * kv + B1M, b_slot(t, kv, 0), b_slot(t, kv, 2), down)

    def b2(t, kv):
        return message(
            t, 7 * kv + B2, b_slot(t, kv, 1 + t), b_slot(t, kv, 3), up if t == 0 else down
        )

    def ax(t, kv, d):
        ref = ak if kv == 0 else av
        return message(t, 7 * kv + AX + d - 1, ref.at[t, 0], ref.at[t, d], line(t, d))

    def pax(t, d):
        return message(t, PAX + d - 1, pa.at[t, d], ra.at[t, d], line(t, -d))

    def pap(t):
        return message(t, PAP, passed.at[t], rap.at[t], mate[t])

    def arrival(t, number, src, dst):
        return message(t, number, src, dst, up)

    def pbf(t):
        return message(t, PBF, pb.at[t, 3], rb.at[t, 0], up if t == 0 else down)

    def pbp(t):
        return message(t, PBP, pb.at[t, 2], rb.at[t, 1], up)

    def pbm(t):
        return message(t, PBM, pb.at[t, 1], rb.at[t, 2], down)

    def each_line(t, act, kv):
        for d in (1, 2, 3):
            pl.when(line_in(t, d))(lambda d=d: act(ax(t, kv, d)))

    def start(m):
        m.start()

    def relay_b(t, kv):
        (b1p if t == 0 else b1m)(t, kv).wait_recv()
        b2(t, kv).start()

    def rest_b(t, kv):
        (b1m if t == 0 else b1p)(t, kv).wait_recv()
        b2(t, kv).wait_recv()

    for t in range(2):
        ap(t, 0).start()
    for t in range(2):
        b1p(t, 0).start()
        b1m(t, 0).start()
    for t in range(2):
        ap(t, 1).start()
    b1p(0, 1).start()
    b1m(0, 1).start()
    for t in range(2):
        ap(t, 0).wait_recv()
        each_line(t, start, 0)
    for t in range(2):
        relay_b(t, 0)
    b1p(1, 1).start()
    b1m(1, 1).start()
    for t in range(2):
        ap(t, 1).wait_recv()
        each_line(t, start, 1)

    y_b = [y, step_y(-2), step_y(2), step_y(4)]
    diff = lax.broadcasted_iota(jnp.int32, (T, T), 1) - lax.broadcasted_iota(jnp.int32, (T, T), 0)

    def threshold(t, d, s, h):
        y_a = partner[t] if h else y
        ahead = 8 * d + (y_a - y_b[s] if t == 0 else y_b[s] - y_a)
        return jnp.where(ahead <= bound_ref[t], -T * ahead, FAR)

    def scores(t):
        @pl.loop(0, lines[t])
        def _(d):
            @pl.when(d > 0)
            def _():
                arrival(t, AX + d - 1, ak.at[t, 0], ak.at[t, d]).wait_recv()

            a = ak[t, d]
            top = jnp.full((1, 2 * T), NEVER, F32)
            for s in range(4):
                dots = lax.dot_general(
                    bk[t, pl.ds(s * T, T)], a, (((1,), (1,)), ((), ())), preferred_element_type=F32
                ) * SCALE
                for h in range(2):
                    gap = diff if t == 0 else -diff
                    piece = jnp.where(
                        gap >= threshold(t, d, s, h), dots[:, h * T : (h + 1) * T], NEVER
                    )
                    sa[pl.ds(s * T, T), pl.ds(h * T, T)] = piece
            for s in range(4):
                top = jnp.maximum(top, jnp.max(sa[pl.ds(s * T, T)], axis=0, keepdims=True))
            top = top.astype(BF16).astype(F32)
            total = jnp.zeros((1, 2 * T), F32)
            for s in range(4):
                w = jnp.exp2(sa[pl.ds(s * T, T)] - top)
                total = total + jnp.sum(w, axis=0, keepdims=True)
                pa_w[t, d, pl.ds(s * T, T)] = w.astype(BF16)
            stat_a[t, d, 0:1] = top
            stat_a[t, d, 1:2] = total
            for s in range(4):
                dots = lax.dot_general(
                    a, bk[t, pl.ds(s * T, T)], (((1,), (1,)), ((), ())), preferred_element_type=F32
                ) * SCALE
                for h in range(2):
                    gap = -diff if t == 0 else diff
                    sb[d, pl.ds(h * T, T), pl.ds(s * T, T)] = jnp.where(
                        gap >= threshold(t, d, s, h), dots[h * T : (h + 1) * T], NEVER
                    )

        top = lax.fori_loop(
            0, lines[t],
            lambda d, m: jnp.maximum(m, jnp.max(sb[d], axis=0, keepdims=True)),
            jnp.full((1, 4 * T), NEVER, F32),
        )
        top = top.astype(BF16).astype(F32)

        def weigh(d, total):
            w = jnp.exp2(sb[d] - top)
            pb_w[t, d] = w.astype(BF16)
            return total + jnp.sum(w, axis=0, keepdims=True)

        total = lax.fori_loop(0, lines[t], weigh, jnp.zeros((1, 4 * T), F32))
        stat_b[t, 0:1] = top
        stat_b[t, 1:2] = total

    for t in range(2):
        rest_b(t, 0)
        scores(t)
        relay_b(t, 1)

    def put(ref, top, total, rows):
        place = lax.broadcasted_iota(jnp.int32, (STAT, rows.shape[1]), 0)
        ref[pl.ds(0, D)] = rows.astype(BF16)
        high = total.astype(BF16).astype(F32)
        stats = jnp.where(place == 0, top, jnp.where(place == 1, high, jnp.where(place == 2, total - high, 0.0)))
        ref[pl.ds(D, STAT)] = stats.astype(BF16)

    def get(ref):
        stats = ref[pl.ds(D, STAT)].astype(F32)
        return stats[0:1], stats[1:2] + stats[2:3], ref[pl.ds(0, D)].astype(F32)

    def b_part(t, s):
        c = pl.ds(s * T, T)
        return stat_b[t, 0:1, c], stat_b[t, 1:2, c], ob[t, :, c]

    def merge(one, two):
        top = jnp.maximum(one[0], two[0])
        a, b = jnp.exp2(one[0] - top), jnp.exp2(two[0] - top)
        return top, one[1] * a + two[1] * b, one[2] * a + two[2] * b

    for t in range(2):
        ob[t] = jnp.zeros_like(ob[t])

        @pl.loop(0, lines[t])
        def _(d, t=t):
            @pl.when(d > 0)
            def _():
                arrival(t, 7 + AX + d - 1, av.at[t, 0], av.at[t, d]).wait_recv()

            values = jnp.concatenate([av[t, d, 0], av[t, d, 1]], axis=1)
            ob[t] += jnp.dot(values, pb_w[t, d], preferred_element_type=F32)

        put(pb.at[t, 3], *b_part(t, 3))
        pbf(t).start()
        put(pb.at[t, 1 + t], *b_part(t, 1 + t))
        (pbm if t == 0 else pbp)(t).start()

    for t in range(2):
        rest_b(t, 1)

        @pl.loop(0, lines[t])
        def _(d, t=t):
            values = jnp.concatenate([bv[t, s] for s in range(4)], axis=1)
            rows = jnp.dot(values, pa_w[t, d], preferred_element_type=F32)

            @pl.when(d == 0)
            def _():
                oa[t] = rows

            @pl.when(d > 0)
            def _():
                put(pa.at[t, d], stat_a[t, d, 0:1], stat_a[t, d, 1:2], rows)
                pax(t, d).start()

    for t in range(2):
        pbf(t).wait_recv()
        put(pb.at[t, 2 - t], *merge(b_part(t, 2 - t), get(rb.at[t, 0])))
        (pbp if t == 0 else pbm)(t).start()

    for t in range(2):

        @pl.loop(1, NX + 1 - lines[t])
        def _(d, t=t):
            arrival(t, PAX + d - 1, pa.at[t, d], ra.at[t, d]).wait_recv()
            top, total, rows = merge((stat_a[t, 0, 0:1], stat_a[t, 0, 1:2], oa[t]), get(ra.at[t, d]))
            stat_a[t, 0, 0:1] = top
            stat_a[t, 0, 1:2] = total
            oa[t] = rows

        put(passed.at[t], stat_a[t, 0, 0:1, T:], stat_a[t, 0, 1:2, T:], oa[t, :, T:])
        pap(t).start()

    def finish(ref, part):
        ref[...] = (part[2] * (1.0 / part[1])).T.astype(BF16)

    for t in range(2):
        pbp(t).wait_recv()
        pbm(t).wait_recv()
        finish(out_b[t], merge(merge(b_part(t, 0), get(rb.at[t, 1])), get(rb.at[t, 2])))
    for t in range(2):
        pap(t).wait_recv()
        own = stat_a[t, 0, 0:1, :T], stat_a[t, 0, 1:2, :T], oa[t, :, :T]
        finish(out_a[t], merge(own, get(rap.at[t])))

    for t in range(2):
        for kv in range(2):
            for m in (ap, b1p, b1m, b2):
                m(t, kv).wait_send()
            each_line(t, lambda m: m.wait_send(), kv)
        for m in (pbf, pbp, pbm, pap):
            m(t).wait_send()

        @pl.loop(1, lines[t])
        def _(d, t=t):
            pax(t, d).wait_send()


def body(left_query, left_value, right_key, right_value, bound):
    hbm = pl.BlockSpec(memory_space=pl.ANY)
    vmem = pl.BlockSpec(memory_space=pltpu.VMEM)
    out = jax.ShapeDtypeStruct((2, T, D), BF16)
    return pl.pallas_call(
        kernel,
        out_shape=(out, out),
        in_specs=[pl.BlockSpec(memory_space=pltpu.SMEM), hbm, hbm, hbm, hbm],
        out_specs=(vmem, vmem),
        scratch_shapes=[
            pltpu.VMEM((2, NX, 2 * T, D), BF16),
            pltpu.VMEM((2, NX, 2, D, T), BF16),
            pltpu.VMEM((2, 4 * T, D), BF16),
            pltpu.VMEM((2, 4, D, T), BF16),
            pltpu.VMEM((2, 2, T, D), BF16),
            pltpu.VMEM((2, NX, 4 * T, 2 * T), BF16),
            pltpu.VMEM((2, NX, 2 * T, 4 * T), BF16),
            pltpu.VMEM((4 * T, 2 * T), F32),
            pltpu.VMEM((NX, 2 * T, 4 * T), F32),
            pltpu.VMEM((2, D, 2 * T), F32),
            pltpu.VMEM((2, D, 4 * T), F32),
            pltpu.VMEM((2, NX, 8, 2 * T), F32),
            pltpu.VMEM((2, 8, 4 * T), F32),
            pltpu.VMEM((2, NX, MSG, 2 * T), BF16),
            pltpu.VMEM((2, NX, MSG, 2 * T), BF16),
            pltpu.VMEM((2, MSG, T), BF16),
            pltpu.VMEM((2, MSG, T), BF16),
            pltpu.VMEM((2, 4, MSG, T), BF16),
            pltpu.VMEM((2, 3, MSG, T), BF16),
            pltpu.SemaphoreType.DMA((2 * KINDS,)),
            pltpu.SemaphoreType.DMA((2 * KINDS,)),
            pltpu.SemaphoreType.DMA((8,)),
        ],
        compiler_params=pltpu.CompilerParams(
            collective_id=0, has_side_effects=True, vmem_limit_bytes=48 * 1024 * 1024
        ),
    )(bound, left_query, left_value, right_key, right_value)


def solution(mesh):
    placed = P("rows", "cols", None)
    return jax.shard_map(
        body,
        mesh=mesh,
        in_specs=(placed, placed, placed, placed, P("rows")),
        out_specs=(placed, placed),
        check_vma=False,
    )
```

time: 240 us -> 52.7 us (0.22)
  waiting for transfers between devices: 202 us -> 0 us
  Pallas kernels: 0 us -> 45.7 us
  between operations: 15.4 us -> 0.65 us
  matrix products: 10.8 us -> 0 us
  other arithmetic: 10.5 us -> 0 us
  local copies, waits for them, and re-layouts: 0.88 us -> 5.58 us
    all_gather x2 -> x0, waiting for transfers between devices: 202 us -> none  [in_one_piece(): filled, at, done = (lax.all_gather(both, axis, axis=dim, tiled=True), 0, [])]
    pallas_call x0 -> x1, Pallas kernels: none -> 45.7 us  [body(): pl.pallas_call(kernel, out_shape=(out, out), in_specs=[pl.BlockSpec(memor...]
    dot_general x4 -> x0, matrix products: 10.8 us -> none  [the longest x2 8.21 us: compute(): jnp.einsum('rid,rjd->rij', mine, other_rows, preferred_element_type=jnp.f...]
    unnamed x2 -> x12, local copies, waits for them, and re-layouts: 0.01 us -> 5.58 us
    concatenate x2 -> x0, other arithmetic: 3.4 us -> none  [in_one_piece(): both = jnp.concatenate(arrays, axis=along)]
    reduce_sum x2 -> x0, other arithmetic: 2.96 us -> none  [online_update(): new_total = jnp.sum(weights, axis=-1)]
  transfers between devices with their start and end apart: 2 -> 0, of which waited for: 2 -> 0; matrix products, arithmetic and copies ran while one was open for 5% -> 0% of each run, Pallas kernels for 0% -> 0%
where the time goes in v1:
time: 52.7 us; the launch traced here: 51.9 us
  Pallas kernels  45.7 us (87%)
  local copies, waits for them, and re-layouts  5.58 us (11%)
  between operations  0.65 us (1%)
    pallas_call x1, Pallas kernels, body(): pl.pallas_call(kernel, out_shape=(out, out), in_specs=[pl.BlockSpec(memor...  45.7 us
    unnamed x12, local copies, waits for them, and re-layouts  5.58 us

profile of v1, /device:TPU:1, one launch (start us, length us, event | category | flops | bytes accessed | tf_op | source)
XLA Modules:
  0.0 51.9 jit_solution(10773357806157167976)
XLA Ops:
  0.6 0.0 copy-start
  0.6 0.9 %copy-done = bf16[2,128,256]{2,1,0:T(8,128)(2,1)S(1)} copy-done((bf16[2,128,256]{2,1,0:T(8,128)(2,1)S(1)}, bf16[2,128,256]{2,1,0:T(8,128)(2,1)}, u32[]{:S(2)}) %copy-start) | copy-done | bytes 131096
  1.5 0.0 copy-start.1
  1.5 0.9 %copy-done.1 = bf16[2,128,256]{2,1,0:T(8,128)(2,1)S(1)} copy-done((bf16[2,128,256]{2,1,0:T(8,128)(2,1)S(1)}, bf16[2,128,256]{2,1,0:T(8,128)(2,1)}, u32[]{:S(2)}) %copy-start.1) | copy-done | bytes 131096
  2.4 0.0 copy-start.2
  2.4 0.9 %copy-done.2 = bf16[2,128,256]{2,1,0:T(8,128)(2,1)S(1)} copy-done((bf16[2,128,256]{2,1,0:T(8,128)(2,1)S(1)}, bf16[2,128,256]{2,1,0:T(8,128)(2,1)}, u32[]{:S(2)}) %copy-start.2) | copy-done | bytes 131096
  3.3 0.0 copy-start.3
  3.3 0.9 %copy-done.3 = bf16[2,128,256]{2,1,0:T(8,128)(2,1)S(1)} copy-done((bf16[2,128,256]{2,1,0:T(8,128)(2,1)S(1)}, bf16[2,128,256]{2,1,0:T(8,128)(2,1)}, u32[]{:S(2)}) %copy-start.3) | copy-done | bytes 131096
  4.3 0.0 copy-start.4
  4.3 0.7 %copy-done.4 = s32[2]{0:T(128)S(1)} copy-done((s32[2]{0:T(128)S(1)}, s32[2]{0:T(128)}, u32[]{:S(2)}) %copy-start.4) | copy-done | bytes 32
  4.9 45.7 %shard_map.68 = (bf16[2,128,256]{2,1,0:T(8,128)(2,1)S(1)}, bf16[2,128,256]{2,1,0:T(8,128)(2,1)S(1)}) custom-call(s32[2]{0:T(128)S(1)} %copy-done.4, bf16[2,128,256]{2,1,0:T(8,128)(2,1)S(1)} %copy-done, bf16[2,128,256]{2,1,0:T(8,128)(2,1)S(1)} %copy-done.1, bf16[2,128,256]{2,1,0:T(8,128)(2,1)S(1)} %copy-done.2, bf16[2,128,256]{2,1,0:T(8,128)(2,1)S(1)} %copy-done.3), custom_call_target="tpu_custom_call" | custom-call | tf_op jit(solution)/shard_map/pallas_call | solution.py:331
  50.6 0.7 %copy.9 = bf16[2,128,256]{2,1,0:T(8,128)(2,1)} copy(bf16[2,128,256]{2,1,0:T(8,128)(2,1)S(1)} %get-tuple-element.4) | data formatting | bytes 262144
  51.3 0.7 %copy.10 = bf16[2,128,256]{2,1,0:T(8,128)(2,1)} copy(bf16[2,128,256]{2,1,0:T(8,128)(2,1)S(1)} %get-tuple-element.5) | data formatting | bytes 262144
Async XLA Ops:
  0.6 0.9 %copy-start = (bf16[2,128,256]{2,1,0:T(8,128)(2,1)S(1)}, bf16[2,128,256]{2,1,0:T(8,128)(2,1)}, u32[]{:S(2)}) copy-start(bf16[2,128,256]{2,1,0:T(8,128)(2,1)} %lq.1) | copy-start | bytes 393220
  1.5 0.9 %copy-start.1 = (bf16[2,128,256]{2,1,0:T(8,128)(2,1)S(1)}, bf16[2,128,256]{2,1,0:T(8,128)(2,1)}, u32[]{:S(2)}) copy-start(bf16[2,128,256]{2,1,0:T(8,128)(2,1)} %lv.1) | copy-start | bytes 393220
  2.4 0.9 %copy-start.2 = (bf16[2,128,256]{2,1,0:T(8,128)(2,1)S(1)}, bf16[2,128,256]{2,1,0:T(8,128)(2,1)}, u32[]{:S(2)}) copy-start(bf16[2,128,256]{2,1,0:T(8,128)(2,1)} %rk.1) | copy-start | bytes 393220
  3.3 0.9 %copy-start.3 = (bf16[2,128,256]{2,1,0:T(8,128)(2,1)S(1)}, bf16[2,128,256]{2,1,0:T(8,128)(2,1)}, u32[]{:S(2)}) copy-start(bf16[2,128,256]{2,1,0:T(8,128)(2,1)} %rv.1) | copy-start | bytes 393220
  4.3 0.7 %copy-start.4 = (s32[2]{0:T(128)S(1)}, s32[2]{0:T(128)}, u32[]{:S(2)}) copy-start(s32[2]{0:T(128)} %bound_ref.1) | copy-start | bytes 28

commit v2 on v1

--- a/solution.py
+++ b/solution.py
@@ -17,15 +17,16 @@
 FAR = 1 << 28
 SCALE = 1.4426950408889634 / 16.0
 
-AP, B1P, B1M, B2, AX = 0, 1, 2, 3, 4
-PAX, PAP, PBF, PBP, PBM = 14, 17, 18, 19, 20
-KINDS = 21
+AP, B1P, B1M, B2P, B2M, AX = 0, 1, 2, 3, 4, 5
+VALUES = 8
+PAX, PAP, PBF, PBP, PBM = 16, 22, 23, 24, 25
+KINDS = 26
 
 
 def kernel(
-    bound_ref, lq, lv, rk, rv, lo, ro,
+    bound, lq, lv, rk, rv, out,
     ak, av, bk, bv, raw, pa_w, pb_w, sa, sb, oa, ob, stat_a, stat_b,
-    pa, ra, passed, rap, pb, rb, send, recv, local,
+    pa, ra, passed, rap, pb, rb, bound_ref, send, recv, local,
 ):
     row = lax.axis_index("rows")
     col = lax.axis_index("cols")
@@ -45,7 +46,7 @@
 
     keys_a, keys_b = (lq.at[0], rk.at[1]), (rk.at[0], lq.at[1])
     vals_a, vals_b = (lv.at[0], rv.at[1]), (rv.at[0], lv.at[1])
-    out_a, out_b = (lo.at[0], ro.at[1]), (ro.at[0], lo.at[1])
+    out_a, out_b = (out.at[0], out.at[3]), (out.at[2], out.at[1])
     lines = [NX - x, x + 1]
 
     barrier = pltpu.get_barrier_semaphore()
@@ -62,12 +63,8 @@
         ):
             copies.append(pltpu.make_async_copy(src, dst, local.at[len(copies)]))
             copies[-1].start()
-    for copy in copies:
-        copy.wait()
-    for t in range(2):
-        av[t, 0, 0] = raw[t, 0].astype(F32).T.astype(BF16)
-        bv[t, 0] = raw[t, 1].astype(F32).T.astype(BF16)
-
+    copies.append(pltpu.make_async_copy(bound, bound_ref, local.at[8]))
+    copies[-1].start()
     pl.semaphore_wait(barrier, 7)
 
     def message(t, number, src, dst, device):
@@ -85,29 +82,38 @@
 
     def ap(t, kv):
         if kv == 0:
-            return message(t, AP, ak.at[t, 0, pl.ds(0, T)], ak.at[t, 0, pl.ds(T, T)], mate[t])
-        return message(t, 7 + AP, av.at[t, 0, 0], av.at[t, 0, 1], mate[t])
+            return message(t, AP, keys_a[t], ak.at[t, 0, pl.ds(T, T)], mate[t])
+        return message(t, VALUES + AP, av.at[t, 0, 0], av.at[t, 0, 1], mate[t])
 
     def b_slot(t, kv, s):
         return bk.at[t, pl.ds(s * T, T)] if kv == 0 else bv.at[t, s]
 
+    def b_own(t, kv):
+        return keys_b[t] if kv == 0 else bv.at[t, 0]
+
     def b1p(t, kv):
-        return message(t, 7 * kv + B1P, b_slot(t, kv, 0), b_slot(t, kv, 1), up)
+        return message(t, VALUES * kv + B1P, b_own(t, kv), b_slot(t, kv, 1), up)
 
     def b1m(t, kv):
-        return message(t, 7 * kv + B1M, b_slot(t, kv, 0), b_slot(t, kv, 2), down)
-
-    def b2(t, kv):
-        return message(
-            t, 7 * kv + B2, b_slot(t, kv, 1 + t), b_slot(t, kv, 3), up if t == 0 else down
-        )
+        return message(t, VALUES * kv + B1M, b_own(t, kv), b_slot(t, kv, 2), down)
+
+    def b_half(t, kv, s, half):
+        if kv == 0:
+            return bk.at[t, pl.ds(s * T + half * (T // 2), T // 2)]
+        return bv.at[t, s, pl.ds(half * (D // 2), D // 2)]
+
+    def b2p(t, kv):
+        return message(t, VALUES * kv + B2P, b_half(t, kv, 1, 0), b_half(t, kv, 3, 0), up)
+
+    def b2m(t, kv):
+        return message(t, VALUES * kv + B2M, b_half(t, kv, 2, 1), b_half(t, kv, 3, 1), down)
 
     def ax(t, kv, d):
         ref = ak if kv == 0 else av
-        return message(t, 7 * kv + AX + d - 1, ref.at[t, 0], ref.at[t, d], line(t, d))
-
-    def pax(t, d):
-        return message(t, PAX + d - 1, pa.at[t, d], ra.at[t, d], line(t, -d))
+        return message(t, VALUES * kv + AX + d - 1, ref.at[t, 0], ref.at[t, d], line(t, d))
+
+    def pax(t, d, h):
+        return message(t, PAX + 3 * h + d - 1, pa.at[t, d, h], ra.at[t, d, h], line(t, -d))
 
     def pap(t):
         return message(t, PAP, passed.at[t], rap.at[t], mate[t])
@@ -131,33 +137,33 @@
     def start(m):
         m.start()
 
+    def load():
+        for copy in copies:
+            copy.wait()
+        for t in range(2):
+            av[t, 0, 0] = raw[t, 0].astype(F32).T.astype(BF16)
+            bv[t, 0] = raw[t, 1].astype(F32).T.astype(BF16)
+
+    def send_a(t, kv):
+        ap(t, kv).start()
+
+    def send_b(t, kv):
+        b1p(t, kv).start()
+        b1m(t, kv).start()
+
+    def relay_a(t, kv):
+        ap(t, kv).wait_recv()
+        each_line(t, start, kv)
+
     def relay_b(t, kv):
-        (b1p if t == 0 else b1m)(t, kv).wait_recv()
-        b2(t, kv).start()
+        b1p(t, kv).wait_recv()
+        b2p(t, kv).start()
+        b1m(t, kv).wait_recv()
+        b2m(t, kv).start()
 
     def rest_b(t, kv):
-        (b1m if t == 0 else b1p)(t, kv).wait_recv()
-        b2(t, kv).wait_recv()
-
-    for t in range(2):
-        ap(t, 0).start()
-    for t in range(2):
-        b1p(t, 0).start()
-        b1m(t, 0).start()
-    for t in range(2):
-        ap(t, 1).start()
-    b1p(0, 1).start()
-    b1m(0, 1).start()
-    for t in range(2):
-        ap(t, 0).wait_recv()
-        each_line(t, start, 0)
-    for t in range(2):
-        relay_b(t, 0)
-    b1p(1, 1).start()
-    b1m(1, 1).start()
-    for t in range(2):
-        ap(t, 1).wait_recv()
-        each_line(t, start, 1)
+        b2p(t, kv).wait_recv()
+        b2m(t, kv).wait_recv()
 
     y_b = [y, step_y(-2), step_y(2), step_y(4)]
     diff = lax.broadcasted_iota(jnp.int32, (T, T), 1) - lax.broadcasted_iota(jnp.int32, (T, T), 0)
@@ -222,11 +228,6 @@
         stat_b[t, 0:1] = top
         stat_b[t, 1:2] = total
 
-    for t in range(2):
-        rest_b(t, 0)
-        scores(t)
-        relay_b(t, 1)
-
     def put(ref, top, total, rows):
         place = lax.broadcasted_iota(jnp.int32, (STAT, rows.shape[1]), 0)
         ref[pl.ds(0, D)] = rows.astype(BF16)
@@ -247,14 +248,14 @@
         a, b = jnp.exp2(one[0] - top), jnp.exp2(two[0] - top)
         return top, one[1] * a + two[1] * b, one[2] * a + two[2] * b
 
-    for t in range(2):
+    def sums_b(t):
         ob[t] = jnp.zeros_like(ob[t])
 
         @pl.loop(0, lines[t])
         def _(d, t=t):
             @pl.when(d > 0)
             def _():
-                arrival(t, 7 + AX + d - 1, av.at[t, 0], av.at[t, d]).wait_recv()
+                arrival(t, VALUES + AX + d - 1, av.at[t, 0], av.at[t, d]).wait_recv()
 
             values = jnp.concatenate([av[t, d, 0], av[t, d, 1]], axis=1)
             ob[t] += jnp.dot(values, pb_w[t, d], preferred_element_type=F32)
@@ -264,9 +265,7 @@
         put(pb.at[t, 1 + t], *b_part(t, 1 + t))
         (pbm if t == 0 else pbp)(t).start()
 
-    for t in range(2):
-        rest_b(t, 1)
-
+    def sums_a(t):
         @pl.loop(0, lines[t])
         def _(d, t=t):
             values = jnp.concatenate([bv[t, s] for s in range(4)], axis=1)
@@ -278,42 +277,92 @@
 
             @pl.when(d > 0)
             def _():
-                put(pa.at[t, d], stat_a[t, d, 0:1], stat_a[t, d, 1:2], rows)
-                pax(t, d).start()
-
-    for t in range(2):
+                for h in range(2):
+                    c = slice(h * T, (h + 1) * T)
+                    put(pa.at[t, d, h], stat_a[t, d, 0:1, c], stat_a[t, d, 1:2, c], rows[:, c])
+                pax(t, d, 1).start()
+
+    def own_a(t):
+        @pl.loop(1, lines[t])
+        def _(d):
+            pax(t, d, 0).start()
+
+    def pass_b(t):
         pbf(t).wait_recv()
         put(pb.at[t, 2 - t], *merge(b_part(t, 2 - t), get(rb.at[t, 0])))
         (pbp if t == 0 else pbm)(t).start()
 
-    for t in range(2):
+    def add_a(t, h):
+        c = slice(h * T, (h + 1) * T)
 
         @pl.loop(1, NX + 1 - lines[t])
-        def _(d, t=t):
-            arrival(t, PAX + d - 1, pa.at[t, d], ra.at[t, d]).wait_recv()
-            top, total, rows = merge((stat_a[t, 0, 0:1], stat_a[t, 0, 1:2], oa[t]), get(ra.at[t, d]))
-            stat_a[t, 0, 0:1] = top
-            stat_a[t, 0, 1:2] = total
-            oa[t] = rows
-
+        def _(d):
+            arrival(t, PAX + 3 * h + d - 1, pa.at[t, d, h], ra.at[t, d, h]).wait_recv()
+            own = stat_a[t, 0, 0:1, c], stat_a[t, 0, 1:2, c], oa[t, :, c]
+            top, total, rows = merge(own, get(ra.at[t, d, h]))
+            stat_a[t, 0, 0:1, c] = top
+            stat_a[t, 0, 1:2, c] = total
+            oa[t, :, c] = rows
+
+    def pass_a(t):
+        add_a(t, 1)
         put(passed.at[t], stat_a[t, 0, 0:1, T:], stat_a[t, 0, 1:2, T:], oa[t, :, T:])
         pap(t).start()
 
     def finish(ref, part):
         ref[...] = (part[2] * (1.0 / part[1])).T.astype(BF16)
 
-    for t in range(2):
+    def last_b(t):
         pbp(t).wait_recv()
         pbm(t).wait_recv()
         finish(out_b[t], merge(merge(b_part(t, 0), get(rb.at[t, 1])), get(rb.at[t, 2])))
-    for t in range(2):
+    def last_a(t):
+        add_a(t, 0)
         pap(t).wait_recv()
         own = stat_a[t, 0, 0:1, :T], stat_a[t, 0, 1:2, :T], oa[t, :, :T]
         finish(out_a[t], merge(own, get(rap.at[t])))
 
+    send_b(0, 0)
+    send_b(1, 0)
+    send_a(0, 0)
+    send_a(1, 0)
+    load()
+    send_a(0, 1)
+    send_a(1, 1)
+    send_b(0, 1)
+    send_b(1, 1)
+    relay_a(0, 0)
+    relay_a(1, 0)
+    relay_b(0, 0)
+    relay_b(1, 0)
+    relay_a(0, 1)
+    relay_a(1, 1)
+    relay_b(0, 1)
+    relay_b(1, 1)
+    rest_b(0, 0)
+    rest_b(1, 0)
+    scores(0)
+    scores(1)
+    sums_b(0)
+    sums_b(1)
+    rest_b(0, 1)
+    rest_b(1, 1)
+    sums_a(0)
+    sums_a(1)
+    own_a(0)
+    own_a(1)
+    pass_b(0)
+    pass_b(1)
+    pass_a(0)
+    pass_a(1)
+    last_b(0)
+    last_b(1)
+    last_a(0)
+    last_a(1)
+
     for t in range(2):
         for kv in range(2):
-            for m in (ap, b1p, b1m, b2):
+            for m in (ap, b1p, b1m, b2p, b2m):
                 m(t, kv).wait_send()
             each_line(t, lambda m: m.wait_send(), kv)
         for m in (pbf, pbp, pbm, pap):
@@ -321,18 +370,18 @@
 
         @pl.loop(1, lines[t])
         def _(d, t=t):
-            pax(t, d).wait_send()
+            pax(t, d, 0).wait_send()
+            pax(t, d, 1).wait_send()
 
 
 def body(left_query, left_value, right_key, right_value, bound):
     hbm = pl.BlockSpec(memory_space=pl.ANY)
     vmem = pl.BlockSpec(memory_space=pltpu.VMEM)
-    out = jax.ShapeDtypeStruct((2, T, D), BF16)
-    return pl.pallas_call(
+    both = pl.pallas_call(
         kernel,
-        out_shape=(out, out),
-        in_specs=[pl.BlockSpec(memory_space=pltpu.SMEM), hbm, hbm, hbm, hbm],
-        out_specs=(vmem, vmem),
+        out_shape=jax.ShapeDtypeStruct((4, T, D), BF16),
+        in_specs=[hbm] * 5,
+        out_specs=vmem,
         scratch_shapes=[
             pltpu.VMEM((2, NX, 2 * T, D), BF16),
             pltpu.VMEM((2, NX, 2, D, T), BF16),
@@ -347,20 +396,22 @@
             pltpu.VMEM((2, D, 4 * T), F32),
             pltpu.VMEM((2, NX, 8, 2 * T), F32),
             pltpu.VMEM((2, 8, 4 * T), F32),
-            pltpu.VMEM((2, NX, MSG, 2 * T), BF16),
-            pltpu.VMEM((2, NX, MSG, 2 * T), BF16),
+            pltpu.VMEM((2, NX, 2, MSG, T), BF16),
+            pltpu.VMEM((2, NX, 2, MSG, T), BF16),
             pltpu.VMEM((2, MSG, T), BF16),
             pltpu.VMEM((2, MSG, T), BF16),
             pltpu.VMEM((2, 4, MSG, T), BF16),
             pltpu.VMEM((2, 3, MSG, T), BF16),
+            pltpu.SMEM((2,), jnp.int32),
             pltpu.SemaphoreType.DMA((2 * KINDS,)),
             pltpu.SemaphoreType.DMA((2 * KINDS,)),
-            pltpu.SemaphoreType.DMA((8,)),
+            pltpu.SemaphoreType.DMA((9,)),
         ],
         compiler_params=pltpu.CompilerParams(
-            collective_id=0, has_side_effects=True, vmem_limit_bytes=48 * 1024 * 1024
+            collective_id=0, has_side_effects=True, vmem_limit_bytes=56 * 1024 * 1024
         ),
     )(bound, left_query, left_value, right_key, right_value)
+    return both[:2], both[2:]
 
 
 def solution(mesh):

time: 52.7 us -> 47.8 us (0.907)
  the two profiles are of different devices: /device:TPU:1 before, /device:TPU:48 now
where the time goes in v2:
time: 47.8 us; the launch traced here: 47.6 us
  Pallas kernels  45.3 us (95%)
  local copies, waits for them, and re-layouts  1.68 us (4%)
  between operations  0.64 us (1%)
    pallas_call x1, Pallas kernels, body(): pl.pallas_call(kernel, out_shape=jax.ShapeDtypeStruct((4, T, D), BF16), i...  45.3 us
    slice x1, local copies, waits for them, and re-layouts, body(): return (both[:2], both[2:])  1.68 us

profile of v2, /device:TPU:48, one launch (start us, length us, event | category | flops | bytes accessed | tf_op | source)
XLA Modules:
  0.0 47.6 jit_solution(15436190233193001728)
XLA Ops:
  0.6 45.3 %shard_map.68 = bf16[4,128,256]{2,1,0:T(8,128)(2,1)} custom-call(s32[2]{0:T(128)} %bound.1, bf16[2,128,256]{2,1,0:T(8,128)(2,1)} %lq.1, bf16[2,128,256]{2,1,0:T(8,128)(2,1)} %lv.1, bf16[2,128,256]{2,1,0:T(8,128)(2,1)} %rk.1, bf16[2,128,256]{2,1,0:T(8,128)(2,1)} %rv.1), custom_call_target="tpu_custom_call" | custom-call | tf_op jit(solution)/shard_map/pallas_call | solution.py:380
  46.0 1.7 %fusion = (bf16[2,128,256]{2,1,0:T(8,128)(2,1)}, bf16[2,128,256]{2,1,0:T(8,128)(2,1)}) fusion(bf16[4,128,256]{2,1,0:T(8,128)(2,1)} %shard_map.68), kind=kLoop, calls=%fused_computation | loop fusion | bytes 524288 | tf_op jit(solution)/shard_map/slice | solution.py:414

commit v3 on v2

--- a/solution.py
+++ b/solution.py
@@ -18,9 +18,9 @@
 SCALE = 1.4426950408889634 / 16.0
 
 AP, B1P, B1M, B2P, B2M, AX = 0, 1, 2, 3, 4, 5
-VALUES = 8
-PAX, PAP, PBF, PBP, PBM = 16, 22, 23, 24, 25
-KINDS = 26
+VALUES = 11
+PAX, PAP, PBF, PBP, PBM = 22, 28, 29, 30, 31
+KINDS = 32
 
 
 def kernel(
@@ -108,9 +108,18 @@
     def b2m(t, kv):
         return message(t, VALUES * kv + B2M, b_half(t, kv, 2, 1), b_half(t, kv, 3, 1), down)
 
-    def ax(t, kv, d):
-        ref = ak if kv == 0 else av
-        return message(t, VALUES * kv + AX + d - 1, ref.at[t, 0], ref.at[t, d], line(t, d))
+    def a_half(t, kv, d, h):
+        return ak.at[t, d, pl.ds(h * T, T)] if kv == 0 else av.at[t, d, h]
+
+    def ax(t, kv, d, h):
+        src = keys_a[t] if kv == 0 and h == 0 else a_half(t, kv, 0, h)
+        return message(t, VALUES * kv + AX + 3 * h + d - 1, src, a_half(t, kv, d, h), line(t, d))
+
+    def arrive_a(t, kv, d):
+        for h in range(2):
+            arrival(
+                t, VALUES * kv + AX + 3 * h + d - 1, a_half(t, kv, 0, h), a_half(t, kv, d, h)
+            ).wait_recv()
 
     def pax(t, d, h):
         return message(t, PAX + 3 * h + d - 1, pa.at[t, d, h], ra.at[t, d, h], line(t, -d))
@@ -130,9 +139,9 @@
     def pbm(t):
         return message(t, PBM, pb.at[t, 1], rb.at[t, 2], down)
 
-    def each_line(t, act, kv):
+    def each_line(t, act, kv, h):
         for d in (1, 2, 3):
-            pl.when(line_in(t, d))(lambda d=d: act(ax(t, kv, d)))
+            pl.when(line_in(t, d))(lambda d=d: act(ax(t, kv, d, h)))
 
     def start(m):
         m.start()
@@ -153,7 +162,10 @@
 
     def relay_a(t, kv):
         ap(t, kv).wait_recv()
-        each_line(t, start, kv)
+        each_line(t, start, kv, 1)
+
+    def send_x(t, kv):
+        each_line(t, start, kv, 0)
 
     def relay_b(t, kv):
         b1p(t, kv).wait_recv()
@@ -178,7 +190,7 @@
         def _(d):
             @pl.when(d > 0)
             def _():
-                arrival(t, AX + d - 1, ak.at[t, 0], ak.at[t, d]).wait_recv()
+                arrive_a(t, 0, d)
 
             a = ak[t, d]
             top = jnp.full((1, 2 * T), NEVER, F32)
@@ -255,13 +267,15 @@
         def _(d, t=t):
             @pl.when(d > 0)
             def _():
-                arrival(t, VALUES + AX + d - 1, av.at[t, 0], av.at[t, d]).wait_recv()
+                arrive_a(t, 1, d)
 
             values = jnp.concatenate([av[t, d, 0], av[t, d, 1]], axis=1)
             ob[t] += jnp.dot(values, pb_w[t, d], preferred_element_type=F32)
 
         put(pb.at[t, 3], *b_part(t, 3))
         pbf(t).start()
+
+    def direct_b(t):
         put(pb.at[t, 1 + t], *b_part(t, 1 + t))
         (pbm if t == 0 else pbp)(t).start()
 
@@ -322,21 +336,29 @@
         own = stat_a[t, 0, 0:1, :T], stat_a[t, 0, 1:2, :T], oa[t, :, :T]
         finish(out_a[t], merge(own, get(rap.at[t])))
 
+    def left_b(t, kv):
+        b1p(t, kv).wait_send()
+        b1m(t, kv).wait_send()
+
     send_b(0, 0)
     send_b(1, 0)
     send_a(0, 0)
     send_a(1, 0)
+    send_x(0, 0)
+    send_x(1, 0)
     load()
     send_a(0, 1)
     send_a(1, 1)
+    send_x(0, 1)
+    send_x(1, 1)
     send_b(0, 1)
     send_b(1, 1)
     relay_a(0, 0)
     relay_a(1, 0)
+    relay_a(0, 1)
+    relay_a(1, 1)
     relay_b(0, 0)
     relay_b(1, 0)
-    relay_a(0, 1)
-    relay_a(1, 1)
     relay_b(0, 1)
     relay_b(1, 1)
     rest_b(0, 0)
@@ -351,6 +373,8 @@
     sums_a(1)
     own_a(0)
     own_a(1)
+    direct_b(0)
+    direct_b(1)
     pass_b(0)
     pass_b(1)
     pass_a(0)
@@ -364,7 +388,8 @@
         for kv in range(2):
             for m in (ap, b1p, b1m, b2p, b2m):
                 m(t, kv).wait_send()
-            each_line(t, lambda m: m.wait_send(), kv)
+            for h in range(2):
+                each_line(t, lambda m: m.wait_send(), kv, h)
         for m in (pbf, pbp, pbm, pap):
             m(t).wait_send()
 

time: 47.8 us -> 47 us (0.983)
  the two profiles are of different devices: /device:TPU:48 before, /device:TPU:24 now
where the time goes in v3:
time: 47 us; the launch traced here: 46.8 us
  Pallas kernels  44.4 us (94%)
  local copies, waits for them, and re-layouts  1.68 us (4%)
  between operations  0.64 us (1%)
    pallas_call x1, Pallas kernels, body(): pl.pallas_call(kernel, out_shape=jax.ShapeDtypeStruct((4, T, D), BF16), i...  44.4 us
    slice x1, local copies, waits for them, and re-layouts, body(): return (both[:2], both[2:])  1.68 us

profile of v3, /device:TPU:24, one launch (start us, length us, event | category | flops | bytes accessed | tf_op | source)
XLA Modules:
  0.0 46.8 jit_solution(7222706304551984808)
XLA Ops:
  0.6 44.4 %shard_map.68 = bf16[4,128,256]{2,1,0:T(8,128)(2,1)} custom-call(s32[2]{0:T(128)} %bound.1, bf16[2,128,256]{2,1,0:T(8,128)(2,1)} %lq.1, bf16[2,128,256]{2,1,0:T(8,128)(2,1)} %lv.1, bf16[2,128,256]{2,1,0:T(8,128)(2,1)} %rk.1, bf16[2,128,256]{2,1,0:T(8,128)(2,1)} %rv.1), custom_call_target="tpu_custom_call" | custom-call | tf_op jit(solution)/shard_map/pallas_call | solution.py:405
  45.1 1.7 %fusion = (bf16[2,128,256]{2,1,0:T(8,128)(2,1)}, bf16[2,128,256]{2,1,0:T(8,128)(2,1)}) fusion(bf16[4,128,256]{2,1,0:T(8,128)(2,1)} %shard_map.68), kind=kLoop, calls=%fused_computation | loop fusion | bytes 524288 | tf_op jit(solution)/shard_map/slice | solution.py:439

commit v4 on v3

--- a/solution.py
+++ b/solution.py
@@ -362,10 +362,10 @@
     relay_b(0, 1)
     relay_b(1, 1)
     rest_b(0, 0)
+    scores(0)
+    sums_b(0)
     rest_b(1, 0)
-    scores(0)
     scores(1)
-    sums_b(0)
     sums_b(1)
     rest_b(0, 1)
     rest_b(1, 1)

time: 47 us -> 45.5 us (0.968)
  the two profiles are of different devices: /device:TPU:24 before, /device:TPU:12 now
where the time goes in v4:
time: 45.5 us; the launch traced here: 45.3 us
  Pallas kernels  43 us (95%)
  local copies, waits for them, and re-layouts  1.68 us (4%)
  between operations  0.64 us (1%)
    pallas_call x1, Pallas kernels, body(): pl.pallas_call(kernel, out_shape=jax.ShapeDtypeStruct((4, T, D), BF16), i...  43 us
    slice x1, local copies, waits for them, and re-layouts, body(): return (both[:2], both[2:])  1.68 us

profile of v4, /device:TPU:12, one launch (start us, length us, event | category | flops | bytes accessed | tf_op | source)
XLA Modules:
  0.0 45.3 jit_solution(8749791291183989677)
XLA Ops:
  0.6 43.0 %shard_map.68 = bf16[4,128,256]{2,1,0:T(8,128)(2,1)} custom-call(s32[2]{0:T(128)} %bound.1, bf16[2,128,256]{2,1,0:T(8,128)(2,1)} %lq.1, bf16[2,128,256]{2,1,0:T(8,128)(2,1)} %lv.1, bf16[2,128,256]{2,1,0:T(8,128)(2,1)} %rk.1, bf16[2,128,256]{2,1,0:T(8,128)(2,1)} %rv.1), custom_call_target="tpu_custom_call" | custom-call | tf_op jit(solution)/shard_map/pallas_call | solution.py:405
  43.6 1.7 %fusion = (bf16[2,128,256]{2,1,0:T(8,128)(2,1)}, bf16[2,128,256]{2,1,0:T(8,128)(2,1)}) fusion(bf16[4,128,256]{2,1,0:T(8,128)(2,1)} %shard_map.68), kind=kLoop, calls=%fused_computation | loop fusion | bytes 524288 | tf_op jit(solution)/shard_map/slice | solution.py:439

commit v5 on v4

--- a/solution.py
+++ b/solution.py
@@ -192,6 +192,36 @@
             def _():
                 arrive_a(t, 0, d)
 
+            a = ak[t, d]
+            for s in range(4):
+                dots = lax.dot_general(
+                    a, bk[t, pl.ds(s * T, T)], (((1,), (1,)), ((), ())), preferred_element_type=F32
+                ) * SCALE
+                for h in range(2):
+                    gap = -diff if t == 0 else diff
+                    sb[d, pl.ds(h * T, T), pl.ds(s * T, T)] = jnp.where(
+                        gap >= threshold(t, d, s, h), dots[h * T : (h + 1) * T], NEVER
+                    )
+
+        top = lax.fori_loop(
+            0, lines[t],
+            lambda d, m: jnp.maximum(m, jnp.max(sb[d], axis=0, keepdims=True)),
+            jnp.full((1, 4 * T), NEVER, F32),
+        )
+        top = top.astype(BF16).astype(F32)
+
+        def weigh(d, total):
+            w = jnp.exp2(sb[d] - top)
+            pb_w[t, d] = w.astype(BF16)
+            return total + jnp.sum(w, axis=0, keepdims=True)
+
+        total = lax.fori_loop(0, lines[t], weigh, jnp.zeros((1, 4 * T), F32))
+        stat_b[t, 0:1] = top
+        stat_b[t, 1:2] = total
+
+    def scores_a(t):
+        @pl.loop(0, lines[t])
+        def _(d):
             a = ak[t, d]
             top = jnp.full((1, 2 * T), NEVER, F32)
             for s in range(4):
@@ -214,31 +244,6 @@
                 pa_w[t, d, pl.ds(s * T, T)] = w.astype(BF16)
             stat_a[t, d, 0:1] = top
             stat_a[t, d, 1:2] = total
-            for s in range(4):
-                dots = lax.dot_general(
-                    a, bk[t, pl.ds(s * T, T)], (((1,), (1,)), ((), ())), preferred_element_type=F32
-                ) * SCALE
-                for h in range(2):
-                    gap = -diff if t == 0 else diff
-                    sb[d, pl.ds(h * T, T), pl.ds(s * T, T)] = jnp.where(
-                        gap >= threshold(t, d, s, h), dots[h * T : (h + 1) * T], NEVER
-                    )
-
-        top = lax.fori_loop(
-            0, lines[t],
-            lambda d, m: jnp.maximum(m, jnp.max(sb[d], axis=0, keepdims=True)),
-            jnp.full((1, 4 * T), NEVER, F32),
-        )
-        top = top.astype(BF16).astype(F32)
-
-        def weigh(d, total):
-            w = jnp.exp2(sb[d] - top)
-            pb_w[t, d] = w.astype(BF16)
-            return total + jnp.sum(w, axis=0, keepdims=True)
-
-        total = lax.fori_loop(0, lines[t], weigh, jnp.zeros((1, 4 * T), F32))
-        stat_b[t, 0:1] = top
-        stat_b[t, 1:2] = total
 
     def put(ref, top, total, rows):
         place = lax.broadcasted_iota(jnp.int32, (STAT, rows.shape[1]), 0)
@@ -367,6 +372,8 @@
     rest_b(1, 0)
     scores(1)
     sums_b(1)
+    scores_a(0)
+    scores_a(1)
     rest_b(0, 1)
     rest_b(1, 1)
     sums_a(0)

time: 45.5 us -> 46.6 us (1.024)
  the two profiles are of different devices: /device:TPU:12 before, /device:TPU:136 now
where the time goes in v5:
time: 46.6 us; the launch traced here: 46.4 us
  Pallas kernels  44.1 us (95%)
  local copies, waits for them, and re-layouts  1.68 us (4%)
  between operations  0.64 us (1%)
    pallas_call x1, Pallas kernels, body(): pl.pallas_call(kernel, out_shape=jax.ShapeDtypeStruct((4, T, D), BF16), i...  44.1 us
    slice x1, local copies, waits for them, and re-layouts, body(): return (both[:2], both[2:])  1.68 us

profile of v5, /device:TPU:136, one launch (start us, length us, event | category | flops | bytes accessed | tf_op | source)
XLA Modules:
  0.0 46.4 jit_solution(11061620952420389528)
XLA Ops:
  0.6 44.1 %shard_map.68 = bf16[4,128,256]{2,1,0:T(8,128)(2,1)} custom-call(s32[2]{0:T(128)} %bound.1, bf16[2,128,256]{2,1,0:T(8,128)(2,1)} %lq.1, bf16[2,128,256]{2,1,0:T(8,128)(2,1)} %lv.1, bf16[2,128,256]{2,1,0:T(8,128)(2,1)} %rk.1, bf16[2,128,256]{2,1,0:T(8,128)(2,1)} %rv.1), custom_call_target="tpu_custom_call" | custom-call | tf_op jit(solution)/shard_map/pallas_call | solution.py:412
  44.7 1.7 %fusion = (bf16[2,128,256]{2,1,0:T(8,128)(2,1)}, bf16[2,128,256]{2,1,0:T(8,128)(2,1)}) fusion(bf16[4,128,256]{2,1,0:T(8,128)(2,1)} %shard_map.68), kind=kLoop, calls=%fused_computation | loop fusion | bytes 524288 | tf_op jit(solution)/shard_map/slice | solution.py:446
